TPU v7x, 32 devices: a whole 2x2x4 slice. The times are simulated.
32 devices in a mesh: exp: 16 (over z, y, x), hid: 2 (over core).
Axes of the slice: x: 2, y: 2, z: 4, core: 2. Of those that a mesh axis runs over, the one named last changes fastest.
Arguments:
- tokens: bfloat16 [8192, 1280], P(('exp', 'hid')), may hold values from -6 to 6
- norm_one: float32 [1280], replicated, may hold values from 0.5 to 1.5
- w_query: bfloat16 [1280, 1280], P('hid'), may hold values from -0.15625 to 0.15625
- w_key: bfloat16 [1280, 1280], P('hid'), may hold values from -0.15625 to 0.15625
- w_value: bfloat16 [1280, 1280], P('hid'), may hold values from -0.15625 to 0.15625
- w_out: bfloat16 [1280, 1280], P('hid'), may hold values from -0.625 to 0.625
- norm_two: float32 [1280], replicated, may hold values from 0.5 to 1.5
- r_gate: bfloat16 [16, 1280, 896], P('exp', None, 'hid'), may hold values from -0.15625 to 0.15625
- r_up: bfloat16 [16, 1280, 896], P('exp', None, 'hid'), may hold values from -0.15625 to 0.15625
- r_down: bfloat16 [16, 896, 1280], P('exp', 'hid'), may hold values from -0.375 to 0.375
- s_gate: bfloat16 [1280, 896], P(None, 'hid'), may hold values from -0.15625 to 0.15625
- s_up: bfloat16 [1280, 896], P(None, 'hid'), may hold values from -0.15625 to 0.15625
- s_down: bfloat16 [896, 1280], P('hid'), may hold values from -0.375 to 0.375
- logits: float32 [8192, 7], P(('exp', 'hid')), may hold values from -3 to 3
- routes: int32 [8192, 7], P(('exp', 'hid')), may hold values from 0 to 14, all different within a row; in each aligned block of 256 rows (0 to 255, 256 to 511, ...) at most 216 rows name the same one
- lengths: int32 [32], P(('exp', 'hid')), may hold values from 64 to 256, as said below
- cotangent: bfloat16 [8192, 1280], P(('exp', 'hid')), may hold values from -6 to 6
Outputs:
- mixed_out: bfloat16 [8192, 1280], P(('exp', 'hid'))
- grad_tokens: bfloat16 [8192, 1280], P(('exp', 'hid'))
- grad_norm_one: float32 [1280], replicated
- grad_query: float32 [1280, 1280], P('hid')
- grad_key: float32 [1280, 1280], P('hid')
- grad_value: float32 [1280, 1280], P('hid')
- grad_wout: float32 [1280, 1280], P('hid')
- grad_norm_two: float32 [1280], replicated
- grad_rgate: float32 [16, 1280, 896], P('exp', None, 'hid')
- grad_rup: float32 [16, 1280, 896], P('exp', None, 'hid')
- grad_rdown: float32 [16, 896, 1280], P('exp', 'hid')
- grad_sgate: float32 [1280, 896], P(None, 'hid')
- grad_sup: float32 [1280, 896], P(None, 'hid')
- grad_sdown: float32 [896, 1280], P('hid')
- grad_logits: float32 [8192, 7], P(('exp', 'hid'))
- counts: int32 [16], replicated
Inputs may be any that keep to these rules, and one draw needn't show every extreme that they name: `routes`: each row names 7 different routed experts; among the rows of one device no expert is named more than 216 times. `lengths`: some sequence is used to its full length.
All inputs are finite; a program needn't handle non-finite values.
Results may differ from a plain program's by a relative error of at most 0.02.
Values may be sent and summed in bfloat16 or wider, within the bound.
A program may use at most 384 MiB of HBM per device.

v0:
```python
import functools

import jax
import jax.numpy as jnp
import numpy as np
from jax import lax
from jax.experimental import pallas as pl
from jax.experimental.pallas import tpu as pltpu
from jax.sharding import PartitionSpec as P

HEADS = 10
HD = 128
MESH = pl.DeviceIdType.MESH


norm_eps = 1e-06
rotary_base = 10000.0
contract_rows = (((0,), (0,)), ((), ()))
contract_cols = (((1,), (1,)), ((), ()))


def matmul(left_side, right_side):
    return jnp.dot(left_side, right_side, preferred_element_type=jnp.float32)


def outer_rows(left_side, right_side):
    return lax.dot_general(left_side, right_side, contract_rows, preferred_element_type=jnp.float32)


def inner_cols(left_side, right_side):
    return lax.dot_general(left_side, right_side, contract_cols, preferred_element_type=jnp.float32)


class Place:
    def __init__(self, n):
        self.n = n; self.nz = 4; self.m = {16: 2, 64: 4}[n]; m = self.m
        self.e = lax.axis_index("exp"); self.c = lax.axis_index("hid"); c = self.c; e = self.e
        self.s1 = m * m; self.s2 = 1 + c * (m - 1); self.s3 = m - c * (m - 1)
        self.x = e % m; self.y = (e // m) % m
        self.c1 = e // self.s1; self.c2 = (e // self.s2) % m; self.c3 = (e // self.s3) % m
    def chip(self, z, y, x): return z * self.s1 + y * self.m + x
    def block(self, z, y): return z * self.m + y
    def others(self):
        far = [((self.c1 + i) % self.nz, (self.y + j) % self.m) for i in range(self.nz) for j in range(self.m)]
        return far[1:]
    def blk(self, a, b, d): return a * self.s1 + b * self.s2 + d * self.s3
    def o2(self): return [(self.c2 + j) % self.m for j in range(1, self.m)]
    def o3(self): return [(self.c3 + j) % self.m for j in range(1, self.m)]
    def greet_all(self):
        barrier = pltpu.get_barrier_semaphore()

        def greet(j, carry):
            pl.semaphore_signal(barrier, inc=1, device_id=((self.e + j) % self.n, self.c), device_id_type=MESH)
            return carry

        lax.fori_loop(1, self.n, greet, 0)
        pl.semaphore_signal(barrier, inc=1, device_id=(self.e, 1 - self.c), device_id_type=MESH)
        pl.semaphore_wait(barrier, self.n)


class Gather:
    def __init__(self, pc, src, dst, ssem, rsem, split, base=0):
        self.pc, self.src, self.dst, self.ssem, self.rsem = pc, src, dst, ssem, rsem
        self.split = split; self.sends = []; self.base = base
    def view(self, ref, part):
        R = self.src.shape[0]
        return ref.at[pl.ds(0, self.split)] if part == 0 else ref.at[pl.ds(self.split, R - self.split)]
    def send(self, part, own, b, to, cond=None):
        i = self.base + len(self.sends)
        src = self.view(self.src if own else self.dst.at[b], part)
        cp = pltpu.make_async_remote_copy(src_ref=src, dst_ref=self.view(self.dst.at[b], part), send_sem=self.ssem.at[i], recv_sem=self.rsem.at[part, b], device_id=(to, self.pc.c), device_id_type=MESH)
        self.sends.append((cond, cp))
        if cond is None: cp.start()
        else: pl.when(cond)(cp.start)
    def wait(self, part, b):
        v = self.view(self.dst.at[b], part)
        to = self.pc.blk(self.pc.c1, self.pc.c2, self.pc.o3()[0])
        pltpu.make_async_remote_copy(src_ref=v, dst_ref=v, send_sem=self.ssem.at[0], recv_sem=self.rsem.at[part, b], device_id=(to, self.pc.c), device_id_type=MESH).wait_recv()
    def updown(self, part, own, b):
        pc = self.pc
        self.send(part, own, b, pc.blk(pc.c1 + 1, pc.c2, pc.c3), pc.c1 < pc.nz - 1)
        self.send(part, own, b, pc.blk(pc.c1 - 1, pc.c2, pc.c3), pc.c1 > 0)
    def to2(self, part, own, b):
        pc = self.pc
        for j in pc.o2(): self.send(part, own, b, pc.blk(pc.c1, j, pc.c3))
    def to3(self, part, own, b):
        pc = self.pc
        for j in pc.o3(): self.send(part, own, b, pc.blk(pc.c1, pc.c2, j))
    def start(self):
        e = self.pc.e
        self.to3(0, True, e); self.to2(0, True, e); self.updown(0, True, e)
        if self.split < self.src.shape[0]:
            self.to3(1, True, e); self.to2(1, True, e); self.updown(1, True, e)
    def zarr(self, part, s, up, k2, k3, more):
        pc = self.pc
        a = pc.c1 - s if up else pc.c1 + s
        cond = (pc.c1 >= s) if up else (pc.c1 < pc.nz - s)
        b = pc.blk(a, k2, k3)
        pl.when(cond)(lambda: self.wait(part, b))
        if s < pc.nz - 1:
            if up: self.send(part, False, b, pc.blk(pc.c1 + 1, pc.c2, pc.c3), (pc.c1 >= s) & (pc.c1 < pc.nz - 1))
            else: self.send(part, False, b, pc.blk(pc.c1 - 1, pc.c2, pc.c3), (pc.c1 < pc.nz - s) & (pc.c1 > 0))
        if more:
            for j in pc.o2(): self.send(part, False, b, pc.blk(pc.c1, j, pc.c3), cond)
            for j in pc.o3(): self.send(part, False, b, pc.blk(pc.c1, pc.c2, j), cond)
    def events(self):
        pc = self.pc; ev = []
        def a2(s):
            def go():
                for j in pc.o2():
                    for sg in ((1, -1) if s else (1,)):
                        a = pc.c1 + sg * s
                        cond = None if s == 0 else ((a >= 0) & (a < pc.nz))
                        b = pc.blk(a, j, pc.c3)
                        if cond is None: self.wait(0, b)
                        else: pl.when(cond)(lambda b=b: self.wait(0, b))
                        for k in pc.o3(): self.send(0, False, b, pc.blk(pc.c1, pc.c2, k), cond)
            return go
        def az(s):
            def go():
                self.zarr(0, s, True, pc.c2, pc.c3, True); self.zarr(0, s, False, pc.c2, pc.c3, True)
            return go
        B = self.split < self.src.shape[0]
        def f1():
            for j in pc.o2():
                b = pc.blk(pc.c1, j, pc.c3); self.wait(1, b); self.to3(1, False, b); self.updown(1, False, b)
        def f2():
            for k in pc.o3():
                b = pc.blk(pc.c1, pc.c2, k); self.wait(1, b); self.updown(1, False, b)
        def f3():
            for j in pc.o2():
                for k in pc.o3():
                    b = pc.blk(pc.c1, j, k); self.wait(1, b); self.updown(1, False, b)
        def fz(s):
            def go():
                for k2 in range(pc.m):
                    for k3 in range(pc.m):
                        self.zarr(1, s, True, k2, k3, False); self.zarr(1, s, False, k2, k3, False)
            return go
        ev += [az(1), a2(0)]
        if B: ev += [f1, f2, f3]
        ev += [az(2), a2(1)]
        if B: ev += [fz(1)]
        ev += [az(3), a2(2)]
        if B: ev += [fz(2)]
        ev += [a2(3)]
        if B: ev += [fz(3)]
        def last():
            for a in range(pc.nz):
                for j in range(pc.m):
                    for k in pc.o3(): self.wait(0, pc.blk(a, j, k))
        ev += [last]
        return ev
    def finish(self):
        for cond, cp in self.sends:
            if cond is None: cp.wait_send()
            else: pl.when(cond)(cp.wait_send)


class Lines:
    def __init__(self, pc, src, dst, ssem, rsem):
        self.pc, self.src, self.dst, self.ssem, self.rsem = pc, src, dst, ssem, rsem
        self.places = [(0, way, 0) for way in (1, -1)] + [(0, 0, j) for j in range(1, pc.m)]
        for s in range(1, pc.nz):
            for way in (1, -1):
                self.places += [(s, way, j) for j in range(0 if s < pc.nz - 1 else 1, pc.m)]

    def send(self, place):
        pc = self.pc
        s, way, j = place
        a = pc.c1 - way * s
        b = pc.block(a, pc.y)
        on = pc.c1 + way
        to = pc.chip(on, pc.y, pc.x) if j == 0 else pc.chip(pc.c1, (pc.y + j) % pc.m, pc.x)
        cond = (a >= 0) & (a < pc.nz)
        if j == 0:
            cond = cond & (on >= 0) & (on < pc.nz)
        copy = pltpu.make_async_remote_copy(
            src_ref=self.src if s == 0 else self.dst.at[b], dst_ref=self.dst.at[b],
            send_sem=self.ssem.at[self.places.index(place)], recv_sem=self.rsem.at[b],
            device_id=(to, pc.c), device_id_type=MESH,
        )
        return cond, copy

    def wait(self, b):
        pc = self.pc
        pltpu.make_async_remote_copy(
            src_ref=self.dst.at[b], dst_ref=self.dst.at[b], send_sem=self.ssem.at[0], recv_sem=self.rsem.at[b],
            device_id=(pc.chip(pc.c1, (pc.y + 1) % pc.m, pc.x), pc.c), device_id_type=MESH,
        ).wait_recv()

    def pass_on(self, s):
        for place in self.places:
            if place[0] == s:
                cond, copy = self.send(place)
                pl.when(cond)(copy.start)

    def start(self):
        self.pass_on(0)

    def line(self, s):
        self.wait_line(s)
        self.pass_on(s)

    def wait_line(self, s):
        pc = self.pc
        for way in (1, -1):
            a = pc.c1 - way * s
            pl.when((a >= 0) & (a < pc.nz))(functools.partial(self.wait, pc.block(a, pc.y)))

    def wait_far(self):
        pc = self.pc
        for a in range(pc.nz):
            for j in range(1, pc.m):
                self.wait(pc.block(a, (pc.y + j) % pc.m))

    def finish(self, distances):
        for place in self.places:
            if place[0] in distances:
                cond, copy = self.send(place)
                pl.when(cond)(copy.wait_send)


def run_staggered(first, second, lag):
    for i in range(max(len(first), len(second) + lag)):
        if i < len(first):
            first[i]()
        if lag <= i < len(second) + lag:
            second[i - lag]()


def part_rows(rows):
    return rows - rows // 80 * 16


def front_kernel(
    n,
    x_ref, cot_ref, gain1, gain2, cos_ref, sin_ref, len_ref, logit_ref, route_ref,
    wq, wk, wv, wo, rg, ru, rd, sg, su, sd,
    all_dy, h_all, fq, fk, fv, fo, fg, fu, fd, pg, pu, pd,
    x1_ref, q_ref, k_ref, v_ref, o_ref, p_ref, gates_in, cnt_ref, base_ref, dus_ref, shared_ref,
    wbuf, h_ref, rows_out, turn_ref, shw, act, dg, dup, give, take,
    gs, gr, hs, hr, ls, ws, wr, wl, es, er, gss, grs, ps, pr, qs, qr, us, ur, ul, xs, xr,
):
    pc = Place(n)
    e, c = pc.e, pc.c
    rows, width = x_ref.shape
    half = width // 2
    pc.greet_all()
    x, y, m = pc.x, pc.y, pc.m
    me = pc.block(pc.c1, y)
    gather_dy = Lines(pc, cot_ref, all_dy, gs, gr)
    gather_h = Lines(pc, h_ref, h_all, hs, hr)
    own_dy = pltpu.make_async_copy(cot_ref, all_dy.at[me], ls.at[0])
    own_h = pltpu.make_async_copy(h_ref, h_all.at[me], ls.at[1])
    own_dy.start()
    partner = (e, 1 - c)
    halves = (wq, wk, wv, wo)
    fulls = (fq, fk, fv, fo)

    def swap(i):
        return pltpu.make_async_remote_copy(
            src_ref=halves[i], dst_ref=wbuf.at[i, c], send_sem=ws.at[i], recv_sem=wr.at[i],
            device_id=partner, device_id_type=MESH,
        )

    def own(i):
        return pltpu.make_async_copy(halves[i], wbuf.at[i, c], wl.at[0, i])

    def keep(i):
        return pltpu.make_async_copy(wbuf.at[i], fulls[i], wl.at[1, i])

    experts_other = (fg, fu, fd)

    def expert_swap(i, src):
        return pltpu.make_async_remote_copy(
            src_ref=src, dst_ref=experts_other[i], send_sem=es.at[i], recv_sem=er.at[i],
            device_id=partner, device_id_type=MESH,
        )

    beside = (pg, pu, pd)

    def half_send(i, j, src):
        return pltpu.make_async_remote_copy(
            src_ref=src, dst_ref=beside[i].at[m - j - 1, c], send_sem=ps.at[i, j - 1], recv_sem=pr.at[i, m - j - 1],
            device_id=(pc.chip(pc.c1, y, (x + j) % m), c), device_id_type=MESH,
        )

    def half_on(i, k):
        return pltpu.make_async_remote_copy(
            src_ref=beside[i].at[k, c], dst_ref=beside[i].at[k, c], send_sem=qs.at[i, k], recv_sem=qr.at[i, k],
            device_id=partner, device_id_type=MESH,
        )

    for i in range(4):
        swap(i).start()
        own(i).start()
    shared_halves = (sg, su, sd)

    def shared_swap(i):
        return pltpu.make_async_remote_copy(
            src_ref=shared_halves[i], dst_ref=shw.at[i, c], send_sem=us.at[i], recv_sem=ur.at[i],
            device_id=partner, device_id_type=MESH,
        )

    def shared_own(i):
        return pltpu.make_async_copy(shared_halves[i], shw.at[i, c], ul.at[i])

    for i, routed in enumerate((rg, ru, rd)):
        for j in range(1, m):
            half_send(i, j, routed).start()
    gather_dy.start()
    for i, routed in enumerate((rg, ru, rd)):
        expert_swap(i, routed).start()
        shared_swap(i).start()
        shared_own(i).start()

    lane = lax.broadcasted_iota(jnp.int32, (rows, 128), 1)
    row = lax.broadcasted_iota(jnp.int32, (rows, 128), 0)
    valid = (row < len_ref[0]).astype(jnp.float32)
    soft, routes = route_columns(logit_ref, route_ref, turn_ref)
    dense = jnp.zeros((rows, 128), jnp.float32)
    named = jnp.zeros((rows, 128), jnp.float32)
    for i in range(route_ref.shape[0]):
        hit = lane == routes[:, i : i + 1]
        dense = dense + jnp.where(hit, soft[:, i : i + 1], 0.0)
        named = named + jnp.where(hit, 1.0, 0.0)
    dense = dense * valid
    cnt_ref[...] = jnp.zeros_like(cnt_ref)
    cnt_ref[:, 0:128] = jnp.sum(named * valid, axis=0, keepdims=True)
    turned = dense.T
    for i in range(n):
        rows_out[i] = turned[i : i + 1, :]
    for i in range(m):
        gates_in[me * m + i] = rows_out[me * m + i]

    def gate_send(a, b2):
        return pltpu.make_async_remote_copy(
            src_ref=rows_out.at[pl.ds(pc.block(a, b2) * m, m)], dst_ref=gates_in.at[pl.ds(me * m, m)],
            send_sem=gss.at[a, b2], recv_sem=grs.at[pc.c1, y],
            device_id=(pc.chip(a, b2, x), c), device_id_type=MESH,
        )

    def gate_wait(a, b2):
        at = pl.ds(pc.block(a, b2) * m, m)
        pltpu.make_async_remote_copy(
            src_ref=rows_out.at[at], dst_ref=gates_in.at[at], send_sem=gss.at[a, b2], recv_sem=grs.at[a, b2],
            device_id=(pc.chip(a, b2, x), c), device_id_type=MESH,
        ).wait_recv()

    for a, b2 in pc.others():
        gate_send(a, b2).start()

    xv = x_ref[...].astype(jnp.float32)
    a = (xv * lax.rsqrt(jnp.mean(xv * xv, axis=-1, keepdims=True) + norm_eps) * gain1[...]).astype(jnp.bfloat16)
    cosine, sine = cos_ref[...], sin_ref[...]

    def project(values, i):
        own(i).wait()
        swap(i).wait_recv()
        keep(i).start()
        return matmul(values[:, :half], wbuf[i, 0]) + matmul(values[:, half:], wbuf[i, 1])

    for i, ref in ((0, q_ref), (1, k_ref)):
        flat = project(a, i)
        for hd in range(HEADS):
            part = flat[:, hd * HD : (hd + 1) * HD]
            ref[:, hd * HD : (hd + 1) * HD] = (part * cosine + swap_halves(part) * sine).astype(jnp.bfloat16)
    v_ref[...] = project(a, 2).astype(jnp.bfloat16)
    gather_dy.line(1)
    scale = HD ** (-0.5)
    row_pos = lax.broadcasted_iota(jnp.int32, (rows, rows), 0)
    col_pos = lax.broadcasted_iota(jnp.int32, (rows, rows), 1)
    allowed = (col_pos <= row_pos) & (col_pos < len_ref[0])

    def one_head(hd, carry):
        at = pl.ds(pl.multiple_of(hd * HD, HD), HD)
        scores = jnp.where(allowed, inner_cols(q_ref[:, at], k_ref[:, at]) * scale, -1e30)
        up = jnp.exp(scores - jnp.max(scores, axis=-1, keepdims=True))
        prob = up / jnp.sum(up, axis=-1, keepdims=True)
        p_ref[hd] = prob
        o_ref[:, at] = matmul(prob.astype(jnp.bfloat16), v_ref[:, at]).astype(jnp.bfloat16)
        return carry

    lax.fori_loop(0, HEADS, one_head, 0)
    gather_dy.line(2)
    x1 = xv + project(o_ref[...], 3)
    x1_ref[...] = x1
    h_ref[...] = (x1 * lax.rsqrt(jnp.mean(x1 * x1, axis=-1, keepdims=True) + norm_eps) * gain2[...]).astype(jnp.bfloat16)
    gather_h.start()
    own_h.start()
    for i in range(3, pc.nz):
        gather_dy.line(i)

    for i in range(3):
        shared_own(i).wait()
        shared_swap(i).wait_recv()
    wg, wu, wd = (shw.at[i] for i in range(3))
    h, z = h_ref[...], cot_ref[...]
    for half in range(2):
        g = inner_cols(h, wg[half])
        u = inner_cols(h, wu[half])
        da = inner_cols(z, wd[half])
        sig = jax.nn.sigmoid(g)
        si = g * sig
        act[half] = (si * u).astype(jnp.bfloat16)
        dup[half] = (da * si).astype(jnp.bfloat16)
        dg[half] = (da * u * sig * (1.0 + g * (1.0 - sig))).astype(jnp.bfloat16)

    def grad_swap(i):
        return pltpu.make_async_remote_copy(
            src_ref=give.at[i], dst_ref=take.at[i], send_sem=xs.at[i], recv_sem=xr.at[i],
            device_id=partner, device_id_type=MESH,
        )

    sides = ((dg, h), (dup, h), (act, z))
    for i, (left, right) in enumerate(sides):
        give[i] = outer_rows(left[1 - c], right).astype(jnp.bfloat16)
        grad_swap(i).start()
    base_ref[...] = x1_ref[...] + matmul(act[0], wd[0]) + matmul(act[1], wd[1])
    dus_ref[...] = matmul(dg[0], wg[0]) + matmul(dg[1], wg[1]) + matmul(dup[0], wu[0]) + matmul(dup[1], wu[1])
    hidden = give.shape[1]
    shared_ref[pl.ds(3 * hidden, shared_ref.shape[0] - 3 * hidden)] = jnp.zeros(
        (shared_ref.shape[0] - 3 * hidden, width), jnp.bfloat16
    )
    for i, (left, right) in enumerate(sides):
        part = outer_rows(left[c], right)
        grad_swap(i).wait()
        shared_ref[pl.ds(i * hidden, hidden)] = (part + take[i].astype(jnp.float32)).astype(jnp.bfloat16)
    for k in range(m - 1):
        for i in range(3):
            half_send(i, m - k - 1, sd).wait_recv()
            half_on(i, k).start()
    gather_dy.wait_far()
    for a, b2 in pc.others():
        gate_wait(a, b2)
        gate_send(a, b2).wait_send()
    gather_h.wait_line(1)
    for j in range(1, m):
        gather_h.wait(pc.block(pc.c1, (y + j) % m))
    gather_dy.finish(range(pc.nz))
    gather_h.finish((0,))
    own_dy.wait()
    own_h.wait()
    for i in range(4):
        swap(i).wait_send()
        keep(i).wait()
    for i, shared in enumerate((sg, su, sd)):
        expert_swap(i, shared).wait()
        shared_swap(i).wait_send()
        for k in range(m - 1):
            half_send(i, k + 1, shared).wait_send()
            half_on(i, k).wait_send()
            other = pltpu.make_async_remote_copy(
                src_ref=beside[i].at[k, 1 - c], dst_ref=beside[i].at[k, 1 - c], send_sem=qs.at[i, k], recv_sem=qr.at[i, k],
                device_id=partner, device_id_type=MESH,
            )
            other.wait_recv()


def front(n, x, cot, gain1, gain2, cosine, sine, length, logits, routes, attn_w, routed_w, shared_w):
    rows, width = x.shape
    hidden = shared_w[0].shape[0]
    vmem = pl.BlockSpec(memory_space=pltpu.VMEM)
    hbm = pl.BlockSpec(memory_space=pl.ANY)
    f32, b16 = jnp.float32, jnp.bfloat16
    out = jax.ShapeDtypeStruct
    dma = pltpu.SemaphoreType.DMA
    wide = out((rows, width), b16)
    full = out((2, width // 2, width), b16)
    nz = 4
    m = {16: 2, 64: 4}[n]
    beside = out((m - 1, 2, hidden, width), b16)
    narrow = pltpu.VMEM((2, rows, hidden), b16)
    three = pltpu.VMEM((3, hidden, width), b16)
    return pl.pallas_call(
        functools.partial(front_kernel, n),
        out_shape=(
            out((nz * m, rows, width), b16), out((nz * m, rows, width), b16), full, full, full, full,
            out((hidden, width), b16), out((hidden, width), b16), out((hidden, width), b16), beside, beside, beside,
            out((rows, width), f32), wide, wide, wide, wide, out((HEADS, rows, rows), f32),
            out((n, 1, rows), f32), out((1, width), f32),
            out((rows, width), f32), out((rows, width), f32), out((n * blocked(3 * hidden, n), width), b16),
        ),
        in_specs=[vmem] * 6 + [pl.BlockSpec(memory_space=pltpu.SMEM)] + [vmem] * 2 + [hbm] * 10,
        out_specs=(hbm,) * 12 + (vmem,) * 11,
        scratch_shapes=[
            pltpu.VMEM((4, 2, width // 2, width), b16), pltpu.VMEM((rows, width), b16), pltpu.VMEM((n, 1, rows), f32), pltpu.VMEM((128, rows), f32),
            pltpu.VMEM((3, 2, hidden, width), b16), narrow, narrow, narrow, three, three,
            dma((64,)), dma((nz * m,)), dma((64,)), dma((nz * m,)), dma((2,)), dma((4,)), dma((4,)), dma((2, 4)), dma((3,)), dma((3,)),
            dma((nz, m)), dma((nz, m)), dma((3, m - 1)), dma((3, m - 1)), dma((3, m - 1)), dma((3, m - 1)),
            dma((3,)), dma((3,)), dma((3,)), dma((3,)), dma((3,)),
        ],
        compiler_params=pltpu.CompilerParams(collective_id=0, has_side_effects=True, vmem_limit_bytes=56 * 2**20),
    )(x, cot, gain1, gain2, cosine, sine, length, logits, routes, *attn_w, *routed_w, *shared_w)


def experts_kernel(
    n, slots,
    h_in, dy_hbm, gates_in, rg, ru, rd, xg, xu, xd, pg, pu, pd, shared_hbm,
    scores_in, du_hbm, tg_hbm, tu_hbm, td_hbm, sum_hbm, y_hbm, far_hbm, h_all, part_hbm, xt_hbm, r3_hbm, r1_hbm,
    wbuf, og, ou, od, total_ref, hbuf, dbuf, act, dg, dup, stage, pbuf, rbuf, give, take, keep,
    gate_ref, s_ref, turn_ref, rows_out,
    gs, gr, lsem, ssem, r3sem, r1sem, bsem, wsem, partsem, pbsem, ysem,
    xssem, xrsem, gsend, grecv, osem, psem, scs, scr, room, vs, va, vb, vc,
):
    pc = Place(n)
    nz, m = pc.nz, pc.m
    c1, e, c, x, y = pc.c1, pc.e, pc.c, pc.x, pc.y
    blocks = nz * m
    me = pc.block(c1, y)
    toward = 1 - 2 * (c1 // (nz // 2))
    together = nz - 1
    grads = (og, ou, od)
    own_half = (rg, ru, rd)
    other_half = (xg, xu, xd)
    shared_half = (pg, pu, pd)

    def weight(p, i, half, src):
        return pltpu.make_async_copy(src, wbuf.at[p % 2, i, half], wsem.at[p % 2, i, half])

    def weights_start(p):
        for i in range(3):
            if p < m - 1:
                for half in range(2):
                    weight(p, i, half, shared_half[i].at[p, half]).start()
            else:
                weight(p, i, c, own_half[i]).start()
                weight(p, i, 1 - c, other_half[i]).start()

    weights_start(0)
    weights_start(1)
    hidden = give.shape[1]
    part_rows = keep.shape[0] // n
    fetch_shared = pltpu.make_async_copy(shared_hbm, keep, psem.at[0])
    fetch_shared.start()
    first_h = pltpu.make_async_copy(h_all.at[me], hbuf.at[0], lsem.at[0, 0])
    first_dy = pltpu.make_async_copy(dy_hbm.at[me], dbuf.at[0], lsem.at[1, 0])
    first_h.start()
    first_dy.start()
    pc.greet_all()
    gather = Lines(pc, None, h_all, gs, gr)
    gather.pass_on(1)

    def rows_of(ref, i):
        return ref.at[pl.ds(pl.multiple_of(i * part_rows, 16), part_rows)]

    from_b = (m - 1) * m * nz
    from_c = from_b + (nz - 1) * m
    shared_sum = Scatter(
        pc, ((m, x, 1), (nz, c1, m * m), (m, y, m)), functools.partial(rows_of, keep),
        lambda i, c_at, b_at: rows_of(take, (i * m + c_at) * nz + b_at),
        lambda i, c_at: rows_of(take, from_b + i * m + c_at),
        lambda i: rows_of(take, from_c + i), (vs, va, vb, vc),
    )
    fetch_shared.wait()
    shared_sum.start_plane(0)
    shared_steps = shared_sum.steps()
    sum_store = pltpu.make_async_copy(rows_of(keep, e), sum_hbm, psem.at[0])

    def shared_done():
        sum_store.start()
        shared_sum.finish()
        pl.semaphore_signal(room, inc=1, device_id=(e, 1 - c), device_id_type=MESH)
        sum_store.wait()

    shared_steps = shared_steps + [shared_done]

    def third(ref, i):
        return ref.at[pl.ds(i * hidden, hidden)]
    turn_ref[...] = jnp.zeros_like(turn_ref)
    for i in range(n):
        turn_ref[i : i + 1, :] = gates_in[i]
    gate_ref[...] = turn_ref[...].T
    for total in grads:
        total[...] = jnp.zeros_like(total)
    s_ref[...] = jnp.zeros_like(s_ref)

    def dest(step):
        p, t = step // blocks, step % blocks
        last = (p + 1) // m
        return (c1 + toward * (t // m + last) + nz) % nz, (y + t % m + last) % m

    def load(step, i):
        b = pc.block(*dest(step))
        return (
            pltpu.make_async_copy(h_all.at[b], hbuf.at[i], lsem.at[0, i]),
            pltpu.make_async_copy(dy_hbm.at[b], dbuf.at[i], lsem.at[1, i]),
        )

    def part_load(step, i):
        return pltpu.make_async_copy(part_hbm.at[pc.block(*dest(step))], pbuf.at[i], pbsem.at[i])

    def part_store(slot, b):
        return pltpu.make_async_copy(stage.at[slot], part_hbm.at[b], partsem.at[slot])

    def y_store(slot, a, b2):
        return pltpu.make_async_copy(stage.at[slot, 0], y_hbm.at[a, b2], ysem.at[slot])

    def pair_send(slot, to, dst, sem):
        return pltpu.make_async_remote_copy(
            src_ref=stage.at[slot], dst_ref=dst, send_sem=ssem.at[slot], recv_sem=sem,
            device_id=(to, c), device_id_type=MESH,
        )

    def du_send(slot, to, dst, sem):
        return pltpu.make_async_remote_copy(
            src_ref=stage.at[slot, 1], dst_ref=dst, send_sem=ssem.at[slot], recv_sem=sem,
            device_id=(to, c), device_id_type=MESH,
        )

    def collect(slot, received):
        def fetch(i):
            return pltpu.make_async_copy(received[i][0], rbuf.at[i % 2], bsem.at[i % 2])

        def begin(i):
            src, sem, landed = received[i]
            pltpu.make_async_remote_copy(
                src_ref=landed, dst_ref=landed, send_sem=ssem.at[slot], recv_sem=sem,
                device_id=(e, 1 - c), device_id_type=MESH,
            ).wait_recv()
            fetch(i).start()

        begin(0)
        total_ref[...] = stage[slot, 1].astype(jnp.float32)
        for i in range(len(received)):
            if i + 1 < len(received):
                begin(i + 1)
            fetch(i).wait()
            total_ref[...] += rbuf[i % 2].astype(jnp.float32)

    def from_y(a, whole):
        if whole:
            return [(far_hbm.at[j, a, 1], r3sem.at[j, a], far_hbm.at[j, a]) for j in range(m - 1)]
        return [(r3_hbm.at[j, a], r3sem.at[j, a], r3_hbm.at[j, a]) for j in range(m - 1)]

    def from_z():
        return [(r1_hbm.at[(c1 + j) % nz], r1sem.at[(c1 + j) % nz], r1_hbm.at[(c1 + j) % nz]) for j in range(1, nz)]

    def swaps():
        return [
            pltpu.make_async_remote_copy(
                src_ref=give.at[i], dst_ref=third(take, i), send_sem=xssem.at[i], recv_sem=xrsem.at[i],
                device_id=(e, 1 - c), device_id_type=MESH,
            )
            for i in range(3)
        ]

    def grad_send(p):
        return pltpu.make_async_remote_copy(
            src_ref=keep.at[pl.ds(0, 3 * hidden)], dst_ref=xt_hbm.at[x], send_sem=gsend, recv_sem=grecv.at[x],
            device_id=(pc.chip(c1, y, (x + p + 1) % m), c), device_id_type=MESH,
        )

    def totals():
        return [
            pltpu.make_async_copy(src.at[c], dst, osem.at[i])
            for i, (src, dst) in enumerate(((og, tg_hbm), (ou, tu_hbm), (od, td_hbm)))
        ]

    first_h.wait()
    first_dy.wait()

    def body(step, carry):
        i = step % 2
        slot = step % slots
        p, t = step // blocks, step % blocks
        last = (p + 1) // m
        a, b2 = dest(step)
        b = pc.block(a, b2)
        column = b * m + (x + p + 1) % m
        for at in range(m):
            @pl.when(step == at * blocks)
            def _():
                for k in range(3):
                    for half in range(2):
                        weight(at, k, half, other_half[k]).wait()
                if at >= 1 and at + 1 < m:
                    weights_start(at + 1)

        @pl.when(step > 0)
        def _():
            for copy in load(step, i):
                copy.wait()

        wg, wu, wd = (wbuf.at[p % 2, k] for k in range(3))
        lane = lax.broadcasted_iota(jnp.int32, gate_ref.shape, 1)
        gate = jnp.sum(jnp.where(lane == column, gate_ref[...], 0.0), axis=1, keepdims=True)
        h = hbuf[i]
        dy = dbuf[i].astype(jnp.float32)
        z = (gate * dy).astype(jnp.bfloat16)
        for half in range(2):
            g = inner_cols(h, wg[half])
            u = inner_cols(h, wu[half])
            da = inner_cols(z, wd[half])
            sg = jax.nn.sigmoid(g)
            si = g * sg
            act[half] = (si * u).astype(jnp.bfloat16)
            dup[half] = (da * si).astype(jnp.bfloat16)
            dg[half] = (da * u * sg * (1.0 + g * (1.0 - sg))).astype(jnp.bfloat16)

        before = step - slots
        before_last = ((before + slots * blocks) // blocks - slots + 1) // m

        @pl.when((before >= 0) & (before_last < 1))
        def _():
            part_store(slot, b).wait()

        before_t = (before + slots * blocks) % blocks

        @pl.when((before >= 0) & (before_last >= 1) & (before_t < together * m) & (before_t % m < m - 1))
        def _():
            pair_send(slot, e, far_hbm.at[0, 0], r3sem.at[0, 0]).wait_send()

        @pl.when((before >= 0) & (before_last >= 1) & ((before_t >= together * m) | (before_t % m == m - 1)))
        def _():
            y_store(slot, a, b2).wait()
            du_send(slot, e, r1_hbm.at[0], r1sem.at[0]).wait_send()

        yv = (matmul(act[0], wd[0]) + matmul(act[1], wd[1])).astype(jnp.bfloat16).astype(jnp.float32)
        s = jnp.sum(yv * dy, axis=1, keepdims=True)
        s_ref[...] = jnp.where(lane == column, s, s_ref[...])
        yv = gate * yv
        du = (
            matmul(dg[0], wg[0]) + matmul(dg[1], wg[1]) + matmul(dup[0], wu[0]) + matmul(dup[1], wu[1])
        ).astype(jnp.bfloat16)

        @pl.when(p == 0)
        def _():
            stage[slot, 0] = yv.astype(jnp.bfloat16)
            stage[slot, 1] = du

        @pl.when(p > 0)
        def _():
            part_load(step, i).wait()
            stage[slot, 0] = (yv + pbuf[i, 0].astype(jnp.float32)).astype(jnp.bfloat16)
            stage[slot, 1] = (du.astype(jnp.float32) + pbuf[i, 1].astype(jnp.float32)).astype(jnp.bfloat16)

        @pl.when(last == 0)
        def _():
            part_store(slot, b).start()

        @pl.when((last == 1) & ((t >= together * m) | (t % m == m - 1)))
        def _():
            y_store(slot, a, b2).start()

        for j in range(1, m):
            @pl.when((last == 1) & (t < together * m) & (b2 == (y + j) % m))
            def _():
                pair_send(slot, pc.chip(c1, b2, x), far_hbm.at[m - j - 1, a], r3sem.at[m - j - 1, a]).start()

            @pl.when((last == 1) & (t >= together * m) & (b2 == (y + j) % m))
            def _():
                du_send(slot, pc.chip(c1, b2, x), r3_hbm.at[m - j - 1, a], r3sem.at[m - j - 1, a]).start()

        for k in range(2, nz):
            pl.when(step == (k - 1) * m - 1)(functools.partial(gather.line, k))

        @pl.when(step < m * blocks - 1)
        def _():
            after = step + 1
            next_a, next_b = dest(after)

            @pl.when((after < blocks) & (next_b != y) & (next_a != c1))
            def _():
                gather.wait(pc.block(next_a, next_b))

            for copy in load(after, 1 - i):
                copy.start()

            @pl.when(after >= blocks)
            def _():
                part_load(after, 1 - i).start()

        for half in range(2):
            og[half] += outer_rows(dg[half], h)
            ou[half] += outer_rows(dup[half], h)
            od[half] += outer_rows(act[half], z)

        for k in range(1, m):
            pl.when(step == k - 1)(functools.partial(shared_sum.start_plane, k))
        spread = [(1 + i, i) for i in range(2 * m - 1)] + [(blocks - 2, 2 * m - 1), (blocks - 1, 2 * m)]
        for at, k in spread:
            pl.when(step == at)(shared_steps[k])

        for at in range(m - 1):
            @pl.when(step == (at + 1) * blocks - 1)
            def _():
                if at >= 1:
                    grad_send(at - 1).wait_send()
                for k, total in enumerate(grads):
                    give[k] = total[1 - c].astype(jnp.bfloat16)
                    third(keep, k)[...] = total[c].astype(jnp.bfloat16)
                    total[...] = jnp.zeros_like(total)
                pl.semaphore_wait(room, 1)
                for copy in swaps():
                    copy.start()

            @pl.when(step == (at + 1) * blocks)
            def _():
                for copy in swaps():
                    copy.wait()
                for k in range(3):
                    third(keep, k)[...] = (
                        third(keep, k)[...].astype(jnp.float32) + third(take, k)[...].astype(jnp.float32)
                    ).astype(jnp.bfloat16)
                pl.semaphore_signal(room, inc=1, device_id=(e, 1 - c), device_id_type=MESH)
                grad_send(at).start()

        for k in range(1, nz):
            @pl.when((last == 1) & (t == k * m))
            def _():
                at = (step - 1) % slots
                a1 = (c1 + toward * k + nz) % nz
                collect(at, from_y(a1, k - 1 < together))
                stage[at, 1] = total_ref[...].astype(jnp.bfloat16)
                du_send(at, pc.chip(a1, y, x), r1_hbm.at[c1], r1sem.at[c1]).start()

        return carry

    lax.fori_loop(0, m * blocks, body, 0)
    for i, total in enumerate(grads):
        give[i] = total[1 - c].astype(jnp.bfloat16)
    pl.semaphore_wait(room, 1)
    for copy in swaps():
        copy.start()
    turned = s_ref[...].T
    for i in range(n):
        rows_out[i] = turned[i : i + 1, :]
    for i in range(m):
        scores_in[me * m + i] = rows_out[me * m + i]

    def score_send(a, b2):
        return pltpu.make_async_remote_copy(
            src_ref=rows_out.at[pl.ds(pc.block(a, b2) * m, m)], dst_ref=scores_in.at[pl.ds(me * m, m)],
            send_sem=scs.at[a, b2], recv_sem=scr.at[c1, y],
            device_id=(pc.chip(a, b2, x), c), device_id_type=MESH,
        )

    def score_wait(a, b2):
        at = pl.ds(pc.block(a, b2) * m, m)
        pltpu.make_async_remote_copy(
            src_ref=rows_out.at[at], dst_ref=scores_in.at[at], send_sem=scs.at[a, b2], recv_sem=scr.at[a, b2],
            device_id=(pc.chip(a, b2, x), c), device_id_type=MESH,
        ).wait_recv()

    for a, b2 in pc.others():
        score_send(a, b2).start()
    for copy in swaps():
        copy.wait()
    for i, total in enumerate(grads):
        total[c] += third(take, i)[...].astype(jnp.float32)
    grad_send(m - 2).wait_send()
    for j in range(1, m):
        at = (x + j) % m
        pltpu.make_async_remote_copy(
            src_ref=xt_hbm.at[at], dst_ref=xt_hbm.at[at], send_sem=gsend, recv_sem=grecv.at[at],
            device_id=(pc.chip(c1, y, at), c), device_id_type=MESH,
        ).wait_recv()
        back = pltpu.make_async_copy(xt_hbm.at[at], take.at[pl.ds(0, 3 * hidden)], bsem.at[0])
        back.start()
        back.wait()
        for i, total in enumerate(grads):
            total[c] += third(take, i)[...].astype(jnp.float32)
    for copy in totals():
        copy.start()
    collect((m * blocks - 1) % slots, from_y(c1, nz - 1 < together) + from_z())
    final = pltpu.make_async_copy(total_ref, du_hbm, bsem.at[0])
    final.start()
    final.wait()
    for step in range(m * blocks - slots, m * blocks):
        t = step % blocks
        if t < together * m and t % m < m - 1:
            pair_send(step % slots, e, far_hbm.at[0, 0], r3sem.at[0, 0]).wait_send()
            continue
        y_store(step % slots, c1, y).wait()
        if step < m * blocks - 1:
            du_send(step % slots, e, r1_hbm.at[0], r1sem.at[0]).wait_send()
    for a, b2 in pc.others():
        score_wait(a, b2)
        score_send(a, b2).wait_send()
    gather.finish(range(1, nz))
    for copy in totals():
        copy.wait()


def experts(h, dy, gates, routed_w, other_w, partner_w, shared):
    blocks, rows, width = dy.shape
    n = gates.shape[0]
    hidden = routed_w[0].shape[0]
    nz = 4
    m = {16: 2, 64: 4}[n]
    slots = 4
    vmem = pl.BlockSpec(memory_space=pltpu.VMEM)
    hbm = pl.BlockSpec(memory_space=pl.ANY)
    f32, b16 = jnp.float32, jnp.bfloat16
    out = jax.ShapeDtypeStruct
    dma = pltpu.SemaphoreType.DMA
    grad = pltpu.VMEM((2, hidden, width), f32)
    pair = pltpu.VMEM((2, rows, width), b16)
    narrow = pltpu.VMEM((2, rows, hidden), b16)
    three = pltpu.VMEM((3, hidden, width), b16)
    return pl.pallas_call(
        functools.partial(experts_kernel, n, slots),
        out_shape=(
            out((n, 1, rows), f32), out((rows, width), f32),
            out((hidden, width), f32), out((hidden, width), f32), out((hidden, width), f32),
            out((shared.shape[0] // n, width), b16), out((nz, m, rows, width), b16), out((m - 1, nz, 2, rows, width), b16),
            out((blocks, rows, width), b16), out((blocks, 2, rows, width), b16), out((m, 3 * hidden, width), b16),
            out((m - 1, nz, rows, width), b16), out((nz, rows, width), b16),
        ),
        in_specs=[hbm, hbm, vmem] + [hbm] * 10,
        out_specs=(vmem,) + (hbm,) * 12,
        input_output_aliases={0: 8},
        scratch_shapes=[
            pltpu.VMEM((2, 3, 2, hidden, width), b16), grad, grad, grad,
            pltpu.VMEM((rows, width), f32), pair, pair, narrow, narrow, narrow,
            pltpu.VMEM((slots, 2, rows, width), b16), pltpu.VMEM((2, 2, rows, width), b16), pair, three,
            pltpu.VMEM((max(3 * hidden, shared.shape[0] // n * (n - 1)), width), b16), pltpu.VMEM(shared.shape, b16),
            pltpu.VMEM((rows, 128), f32), pltpu.VMEM((rows, 128), f32), pltpu.VMEM((128, rows), f32), pltpu.VMEM((n, 1, rows), f32),
            dma((64,)), dma((blocks,)), dma((2, 2)), dma((slots,)), dma((m - 1, nz)), dma((nz,)), dma((2,)),
            dma((2, 3, 2)), dma((slots,)), dma((2,)), dma((slots,)),
            dma((3,)), dma((3,)), dma, dma((m,)), dma((3,)), dma((3,)), dma((nz, m)), dma((nz, m)),
            pltpu.SemaphoreType.REGULAR, dma((n,)), dma((m - 1, m, nz)), dma((nz - 1, m)), dma((m - 1,)),
        ],
        compiler_params=pltpu.CompilerParams(collective_id=1, has_side_effects=True, vmem_limit_bytes=62 * 2**20),
    )(h, dy, gates, *routed_w, *other_w, *partner_w, shared)


def swap_halves(values):
    return pltpu.roll(values, HD // 2, axis=1)


def route_columns(logit_ref, route_ref, turn_ref):
    count = logit_ref.shape[0]
    logits = logit_ref[...]
    raised = jnp.exp(logits - jnp.max(logits, axis=0, keepdims=True))
    turn_ref[...] = jnp.zeros_like(turn_ref)
    turn_ref[0:count, :] = raised / jnp.sum(raised, axis=0, keepdims=True)
    soft = turn_ref[...].T
    turn_ref[0:count, :] = route_ref[...].astype(jnp.float32)
    return soft, turn_ref[...].T.astype(jnp.int32)


class Scatter:
    def __init__(self, pc, axes, block, ra, rb, rc, sems):
        self.pc, self.block, self.ra, self.rb, self.rc = pc, block, ra, rb, rc
        (self.na, self.a, self.sa), (self.nb, self.b, self.sb), (self.nc, self.c, self.sc) = axes
        self.ssem, self.sema, self.semb, self.semc = sems

    def at(self, i, j, k):
        a, b, c = (self.a + i) % self.na, (self.b + j) % self.nb, (self.c + k) % self.nc
        return a * self.sa + b * self.sb + c * self.sc

    def copy(self, b, dst, sem, to):
        return pltpu.make_async_remote_copy(
            src_ref=self.block(b), dst_ref=dst, send_sem=self.ssem.at[b], recv_sem=sem,
            device_id=(to, self.pc.c), device_id_type=MESH,
        )

    def add(self, total, src, sem):
        self.copy(self.pc.e, src, sem, self.at(1, 0, 0)).wait_recv()
        return total + src[...].astype(jnp.float32)

    def place_b(self, j):
        return (self.b + j) % self.nb

    def place_c(self, k):
        return (self.c + k) % self.nc

    def start(self):
        for k in range(self.nc):
            self.start_plane(k)

    def start_plane(self, p):
        k = (p + 1) % self.nc
        for i in range(1, self.na):
            for j in list(range(1, self.nb)) + [0]:
                b, c = self.place_b(j), self.place_c(k)
                slot = self.na - i - 1
                self.copy(self.at(i, j, k), self.ra(slot, c, b), self.sema.at[slot, c, b], self.at(i, 0, 0)).start()

    def collect(self, j, k, level):
        block = self.block(self.at(0, j, k))
        b, c = self.place_b(j), self.place_c(k)
        total = block[...].astype(jnp.float32)
        for i in range(self.na - 1):
            total = self.add(total, self.ra(i, c, b), self.sema.at[i, c, b])
        if level >= 2:
            for i in range(self.nb - 1):
                total = self.add(total, self.rb(i, c), self.semb.at[i, c])
        if level >= 3:
            for i in range(self.nc - 1):
                total = self.add(total, self.rc(i), self.semc.at[i])
        block[...] = total.astype(jnp.bfloat16)

    def second(self, p):
        k = (p + 1) % self.nc
        for j in range(1, self.nb):
            self.collect(j, k, 1)
            slot = self.nb - j - 1
            self.copy(self.at(0, j, k), self.rb(slot, self.place_c(k)), self.semb.at[slot, self.place_c(k)], self.at(0, j, 0)).start()

    def third(self, p):
        k = p + 1
        self.collect(0, k, 2)
        slot = self.nc - k - 1
        self.copy(self.at(0, 0, k), self.rc(slot), self.semc.at[slot], self.at(0, 0, k)).start()

    def last(self):
        self.collect(0, 0, 3)

    def steps(self):
        found = [functools.partial(self.second, 0)]
        for p in range(1, self.nc):
            found += [functools.partial(self.second, p), functools.partial(self.third, p - 1)]
        return found + [self.last]

    def finish(self):
        n = self.pc.n

        def one(j, carry):
            to = (self.pc.e + j) % n
            self.copy(to, self.rc(0), self.semc.at[0], to).wait_send()
            return carry

        lax.fori_loop(1, n, one, 0)


def tail_kernel(
    n,
    x_ref, x1_ref, cot_ref, dh_ref, dus_hbm, base_hbm, own_ref, q_ref, k_ref, v_ref, o_ref, p_ref, wq, wk, wv, wo,
    gain1, gain2, cos_ref, sin_ref, cnt_ref, len_ref, logit_ref, route_ref, scores_in, y_hbm, far_hbm,
    out_ref, gtok_ref, glog_ref, small_ref, ag0, ag1, ags, y3_hbm, y1_hbm,
    dx_ref, dq_ref, dk_ref, dv_ref, a_ref, give, take, stack0, stack1, r3, r2, r1,
    sm_core, sm_d3, sm_d2, sm_z,
    wbuf, wsem, turn_ref, ybuf, ytmp,
    gs, gr, ss, s3, s2, s1, xs, xr, cs, cr, locs, yl, yt, ys3, ys1, y3s, y1s,
):
    pc = Place(n)
    c1, c2, c3, e, c, nz, m = pc.c1, pc.c2, pc.c3, pc.e, pc.c, pc.nz, pc.m
    rows, width = x_ref.shape
    half = width // 2
    pc.greet_all()

    x, y = pc.x, pc.y

    def y_far(a, j):
        return pltpu.make_async_remote_copy(
            src_ref=y_hbm.at[a, (y + j) % m], dst_ref=y3_hbm.at[m - j - 1, a], send_sem=ys3.at[j - 1, a], recv_sem=y3s.at[m - j - 1, a],
            device_id=(pc.chip(c1, (y + j) % m, x), c), device_id_type=MESH,
        )

    def y_along(a):
        return pltpu.make_async_remote_copy(
            src_ref=ybuf.at[a], dst_ref=y1_hbm.at[c1], send_sem=ys1.at[a], recv_sem=y1s.at[c1],
            device_id=(pc.chip(a, y, x), c), device_id_type=MESH,
        )

    toward = 1 - 2 * (c1 // (nz // 2))
    together = nz - 1

    def plane(i):
        return (c1 + toward * (i + 1) + nz) % nz

    for i in range(together, nz):
        for j in range(1, m):
            y_far(plane(i), j).start()
    y_own = [pltpu.make_async_copy(y_hbm.at[a, y], ybuf.at[a], yl.at[a]) for a in range(nz)]
    for copy in y_own:
        copy.start()

    def y_sum(a, received):
        def fetched(i):
            return pltpu.make_async_copy(received[i][0], ytmp.at[i % 2], yt.at[i % 2])

        def begin(i):
            src, sem = received[i]
            if sem is not None:
                pltpu.make_async_remote_copy(
                    src_ref=src, dst_ref=src, send_sem=ys1.at[0], recv_sem=sem, device_id=(e, 1 - c), device_id_type=MESH,
                ).wait_recv()
            fetched(i).start()

        begin(0)
        total = ybuf[a].astype(jnp.float32)
        for i in range(len(received)):
            if i + 1 < len(received):
                begin(i + 1)
            fetched(i).wait()
            total = total + ytmp[i % 2].astype(jnp.float32)
        return total

    def y_from3(i):
        a = plane(i)
        if i < together:
            return [(far_hbm.at[k, a, 0], None) for k in range(m - 1)]
        return [(y3_hbm.at[k, a], y3s.at[k, a]) for k in range(m - 1)]

    def y_third(i):
        a = plane(i)
        ybuf[a] = y_sum(a, y_from3(i)).astype(jnp.bfloat16)
        y_along(a).start()

    def y_last():
        along = [(y1_hbm.at[(c1 + j) % nz], y1s.at[(c1 + j) % nz]) for j in range(1, nz)]
        out_ref[...] = (dx_ref[...] + y_sum(c1, y_from3(nz - 1) + along)).astype(jnp.bfloat16)

    def y_finish():
        for i in range(nz - 1):
            y_along(plane(i)).wait_send()
        for i in range(together, nz):
            for j in range(1, m):
                y_far(plane(i), j).wait_send()

    gather_s = Gather(pc, own_ref, ags, gs.at[2], gr.at[2], own_ref.shape[0])
    loc_s = pltpu.make_async_copy(own_ref, ags.at[e], locs.at[2])
    gather_s.start()
    loc_s.start()
    shared_events = gather_s.events()

    def fetch(src, i):
        return pltpu.make_async_copy(src, wbuf.at[i], wsem.at[i])

    get_dus = pltpu.make_async_copy(dus_hbm, dx_ref, locs.at[0])
    get_dus.start()
    fetch(wo, 0).start()
    fetch(wv, 1).start()

    x1 = x1_ref[...]
    up = cot_ref[...].astype(jnp.float32)
    get_dus.wait()
    dh = dh_ref[...] + dx_ref[...]
    r_two = lax.rsqrt(jnp.mean(x1 * x1, axis=-1, keepdims=True) + norm_eps)
    n_two = x1 * r_two
    scaled = dh * gain2[...]
    grad_two = jnp.sum(dh * n_two, axis=0, keepdims=True)
    dx = up + r_two * (scaled - n_two * jnp.mean(scaled * n_two, axis=-1, keepdims=True))
    dx_ref[...] = dx
    dx_low = dx.astype(jnp.bfloat16)

    def columns(ref, which):
        return ref[:, pl.ds(pl.multiple_of(which * half, 128), half)]

    def hand(i):
        return pltpu.make_async_remote_copy(
            src_ref=give.at[i], dst_ref=take.at[i], send_sem=xs.at[i], recv_sem=xr.at[i],
            device_id=(e, 1 - c), device_id_type=MESH,
        )

    def to_partner(i, left, right):
        give[i] = outer_rows(columns(left, 1 - c), right).astype(jnp.bfloat16)
        hand(i).start()

    def own_part(i, left, right, stack, at):
        block = stack.shape[1]
        part = outer_rows(columns(left, c), right)
        hand(i).wait_recv()
        total = (part + take[i].astype(jnp.float32)).astype(jnp.bfloat16)
        stack[pl.ds(at * (half // block), half // block)] = total.reshape(half // block, block, width)

    to_partner(0, o_ref, dx_low)
    shared_events[0]()
    fetch(wo, 0).wait()
    dq_ref[...] = inner_cols(dx_low, wbuf[0]).astype(jnp.bfloat16)
    fetch(wk, 0).start()
    cosine, sine = cos_ref[...], sin_ref[...]
    scale = HD ** (-0.5)

    def one_head(hd, carry):
        at = pl.ds(pl.multiple_of(hd * HD, HD), HD)
        prob = p_ref[hd]
        d_o, val, que, key = dq_ref[:, at], v_ref[:, at], q_ref[:, at], k_ref[:, at]
        dv_ref[:, at] = outer_rows(prob.astype(jnp.bfloat16), d_o).astype(jnp.bfloat16)
        d_prob = inner_cols(d_o, val)
        inner = jnp.sum(prob * d_prob, axis=-1, keepdims=True)
        d_score = (prob * (d_prob - inner)).astype(jnp.bfloat16)
        d_q = matmul(d_score, key) * scale
        d_k = outer_rows(d_score, que) * scale
        dq_ref[:, at] = (d_q * cosine - swap_halves(d_q) * sine).astype(jnp.bfloat16)
        dk_ref[:, at] = (d_k * cosine - swap_halves(d_k) * sine).astype(jnp.bfloat16)
        return carry

    lax.fori_loop(0, HEADS, one_head, 0)
    for copy in y_own:
        copy.wait()
    for i in range(nz - 1):
        y_third(i)
    xv = x_ref[...].astype(jnp.float32)
    r_one = lax.rsqrt(jnp.mean(xv * xv, axis=-1, keepdims=True) + norm_eps)
    n_one = xv * r_one
    a_ref[...] = (n_one * gain1[...]).astype(jnp.bfloat16)
    shared_events[1]()
    to_partner(1, a_ref, dv_ref[...])
    to_partner(2, a_ref, dk_ref[...])
    to_partner(3, a_ref, dq_ref[...])
    if n * stack0.shape[1] > 2 * half:
        stack0[...] = jnp.zeros_like(stack0)
        stack1[...] = jnp.zeros_like(stack1)
    own_part(0, o_ref, dx_low, stack0, 0)
    own_part(1, a_ref, dv_ref[...], stack0, 1)
    first, second = (
        Scatter(
            pc, ((m, c3, pc.s3), (m, c2, pc.s2), (nz, c1, pc.s1)), lambda b, stack=stack: stack.at[b], lambda k, a, b2, i=i: r3.at[i, k, a, b2], lambda k, a, i=i: r2.at[i, k, a],
            lambda k, i=i: r1.at[i, k], (ss.at[i], s3.at[i], s2.at[i], s1.at[i]),
        )
        for i, stack in enumerate((stack0, stack1))
    )
    first.start()
    shared_events[2]()
    shared_events[3]()
    own_part(2, a_ref, dk_ref[...], stack1, 0)
    own_part(3, a_ref, dq_ref[...], stack1, 1)
    second.start()
    fetch(wv, 1).wait()
    da = inner_cols(dv_ref[...], wbuf[1])
    fetch(wq, 1).start()
    fetch(wk, 0).wait()
    da = da + inner_cols(dk_ref[...], wbuf[0])
    fetch(wq, 1).wait()
    da = da + inner_cols(dq_ref[...], wbuf[1])
    scaled_one = da * gain1[...]
    grad_one = jnp.sum(da * n_one, axis=0, keepdims=True)
    back = r_one * (scaled_one - n_one * jnp.mean(scaled_one * n_one, axis=-1, keepdims=True))
    gtok_ref[...] = (dx_ref[...] + back).astype(jnp.bfloat16)
    get_base = pltpu.make_async_copy(base_hbm, dx_ref, wsem.at[0])
    get_base.start()

    def exchange(ref, own, level, peers, value):
        ref[own] = value
        copies = [
            pltpu.make_async_remote_copy(
                src_ref=ref.at[own], dst_ref=ref.at[own], send_sem=cs.at[level, i], recv_sem=cr.at[level, own],
                device_id=to, device_id_type=MESH,
            )
            for i, (to, at) in enumerate(peers)
        ]
        for copy in copies:
            copy.start()

        def done():
            for i, (to, at) in enumerate(peers):
                pltpu.make_async_remote_copy(
                    src_ref=ref.at[own], dst_ref=ref.at[at], send_sem=cs.at[level, i], recv_sem=cr.at[level, at],
                    device_id=to, device_id_type=MESH,
                ).wait_recv()
            for copy in copies:
                copy.wait_send()
            total = ref[0]
            for i in range(1, ref.shape[0]):
                total = total + ref[i]
            return total

        return done

    turn_ref[...] = jnp.zeros_like(turn_ref)
    for i in range(n):
        turn_ref[i : i + 1, :] = scores_in[i]
    scores = turn_ref[...].T
    lane = lax.broadcasted_iota(jnp.int32, (rows, 128), 1)
    row = lax.broadcasted_iota(jnp.int32, (rows, 128), 0)
    scores = jnp.where(row < len_ref[0], scores, 0.0)
    soft, routes = route_columns(logit_ref, route_ref, turn_ref)
    share = jnp.zeros((rows, 128), jnp.float32)
    for i in range(route_ref.shape[0]):
        picked = jnp.sum(jnp.where(lane == routes[:, i : i + 1], scores, 0.0), axis=-1, keepdims=True)
        share = jnp.where(lane == i, picked, share)
    grad_logits = soft * (share - jnp.sum(soft * share, axis=-1, keepdims=True))
    glog_ref[...] = grad_logits.T[0 : route_ref.shape[0], :]

    small = jnp.concatenate([grad_one, grad_two, cnt_ref[...], jnp.zeros((5, width), jnp.float32)], axis=0)
    level0 = exchange(sm_core, c, 0, [((e, 1 - c), 1 - c)], small)
    steps0, steps1 = first.steps(), second.steps()
    steps0[0]()
    steps0[1]()
    shared_events[4]()
    level1 = exchange(sm_d3, c3, 1, [((pc.blk(c1, c2, j), c), j) for j in pc.o3()], level0())
    steps0[2]()
    steps1[0]()
    steps0[3]()
    steps1[1]()
    steps0[4]()
    for event in shared_events[5:-1]:
        event()
    level2 = exchange(sm_d2, c2, 2, [((pc.blk(c1, j, c3), c), j) for j in pc.o2()], level1())
    steps1[2]()
    for step in steps0[5:-1]:
        step()
    level3 = exchange(sm_z, c1, 3, [((pc.blk((c1 + j) % nz, c2, c3), c), (c1 + j) % nz) for j in range(1, nz)], level2())
    for step in steps1[3:-1]:
        step()
    small_ref[...] = level3()
    steps0[-1]()
    g0 = Gather(pc, stack0.at[e], ag0, gs.at[0], gr.at[0], stack0.shape[1])
    g0.start()
    loc0 = pltpu.make_async_copy(stack0.at[e], ag0.at[e], locs.at[0])
    loc0.start()
    steps1[-1]()
    g1 = Gather(pc, stack1.at[e], ag1, gs.at[1], gr.at[1], stack1.shape[1])
    g1.start()
    loc1 = pltpu.make_async_copy(stack1.at[e], ag1.at[e], locs.at[1])
    loc1.start()
    get_base.wait()
    y_last()
    run_staggered(g0.events(), g1.events(), 1)
    shared_events[-1]()
    for g in (gather_s, g0, g1):
        g.finish()
    first.finish()
    second.finish()
    loc_s.wait()
    loc0.wait()
    loc1.wait()
    y_finish()
    for i in range(4):
        hand(i).wait_send()


def tail(n, x, x1, cot, dh, dus, base, own, q, k, v, o, prob, wq, wk, wv, wo, gain1, gain2, cosine, sine, cnt, length, logits, routes, scores, y, far):
    nz = 4
    m = {16: 2, 64: 4}[n]
    rows, width = x.shape
    half = width // 2
    block = blocked(2 * half, n)
    vmem = pl.BlockSpec(memory_space=pltpu.VMEM)
    hbm = pl.BlockSpec(memory_space=pl.ANY)
    f32, b16 = jnp.float32, jnp.bfloat16
    out = jax.ShapeDtypeStruct
    dma = pltpu.SemaphoreType.DMA
    wide = pltpu.VMEM((rows, width), b16)
    return pl.pallas_call(
        functools.partial(tail_kernel, n),
        out_shape=(
            out((rows, width), b16), out((rows, width), b16), out(logits.shape, f32), out((8, width), f32),
            out((n, block, width), b16), out((n, block, width), b16),
            out((n,) + own.shape, b16),
            out((m - 1, nz, rows, width), b16), out((nz, rows, width), b16),
        ),
        in_specs=[vmem] * 4 + [hbm] * 2 + [vmem] * 6 + [hbm] * 4 + [vmem] * 5 + [pl.BlockSpec(memory_space=pltpu.SMEM)] + [vmem] * 3 + [hbm] * 2,
        out_specs=(vmem,) * 4 + (hbm,) * 5,
        scratch_shapes=[
            pltpu.VMEM((rows, width), f32), wide, wide, wide, wide,
            pltpu.VMEM((4, half, width), b16), pltpu.VMEM((4, half, width), b16),
            pltpu.VMEM((n, block, width), b16), pltpu.VMEM((n, block, width), b16),
            pltpu.VMEM((2, m - 1, nz, m, block, width), b16), pltpu.VMEM((2, m - 1, nz, block, width), b16),
            pltpu.VMEM((2, nz - 1, block, width), b16),
            pltpu.VMEM((2, 8, width), f32), pltpu.VMEM((m, 8, width), f32), pltpu.VMEM((m, 8, width), f32), pltpu.VMEM((nz, 8, width), f32),
            pltpu.VMEM((2, width, width), b16), dma((2,)), pltpu.VMEM((128, rows), f32),
            pltpu.VMEM((nz, rows, width), b16), pltpu.VMEM((2, rows, width), b16),
            dma((3, 160)), dma((3, 2, n)), dma((2, n)), dma((2, m - 1, nz, m)), dma((2, m - 1, nz)), dma((2, nz - 1)),
            dma((4,)), dma((4,)), dma((4, max(nz, m))), dma((4, max(nz, m, 2))), dma((3,)),
            dma((nz,)), dma((2,)), dma((m - 1, nz)), dma((nz,)), dma((m - 1, nz)), dma((nz,)),
        ],
        compiler_params=pltpu.CompilerParams(collective_id=2, has_side_effects=True, vmem_limit_bytes=63 * 2**20),
    )(x, x1, cot, dh, dus, base, own, q, k, v, o, prob, wq, wk, wv, wo, gain1, gain2, cosine, sine, cnt, length, logits, routes, scores, y, far)


def blocked(count, n):
    return -(-count // (16 * n)) * 16


def from_blocks(blocks, count):
    return blocks.reshape(-1, blocks.shape[2])[:count].astype(jnp.float32)


def rotary_rows(seq_len):
    position = np.arange(seq_len).astype(np.float32)
    inverse_freq = (rotary_base ** (-2.0 * np.arange(HD // 2).astype(np.float32) / HD)).astype(np.float32)
    angle = position[:, None] * inverse_freq[None, :]
    cosine, sine = np.cos(angle), np.sin(angle)
    return np.concatenate([cosine, cosine], axis=1), np.concatenate([-sine, sine], axis=1)


def on_device(
    tokens, norm_one, w_query, w_key, w_value, w_out, norm_two, r_gate, r_up, r_down, s_gate, s_up, s_down,
    logits, routes, lengths, cotangent,
):
    rows, width = tokens.shape
    n = lax.axis_size("exp")
    hidden = s_gate.shape[1]
    cosine, sine = (jnp.asarray(table) for table in rotary_rows(rows))
    gain1, gain2 = norm_one[None], norm_two[None]
    logits, routes = logits.T, routes.T
    attn_w = (w_query, w_key, w_value, w_out)
    routed_w = (r_gate[0].T, r_up[0].T, r_down[0])
    shared_w = (s_gate.T, s_up.T, s_down)
    (
        all_dy, all_h, fq, fk, fv, fo, fg, fu, fd, pg, pu, pd, mixed, queries, keys_all, values_all, attended, prob, gates, counts,
        base, shared_back, shared_grads,
    ) = front(
        n, tokens, cotangent, gain1, gain2, cosine, sine, lengths, logits, routes,
        attn_w, routed_w, shared_w,
    )
    scores, grad_hidden, tg, tu, td, shared_sum, outs, far_outs = experts(
        all_h, all_dy, gates, routed_w, (fg, fu, fd), (pg, pu, pd), shared_grads
    )[:8]
    full = (width, width)
    output, grad_tokens, grad_logits, small_sums, sum0, sum1, sum_s = tail(
        n, tokens, mixed, cotangent, grad_hidden, shared_back, base, shared_sum, queries, keys_all, values_all, attended, prob,
        fq.reshape(full), fk.reshape(full), fv.reshape(full), fo.reshape(full),
        gain1, gain2, cosine, sine, counts, lengths, logits, routes, scores,
        outs, far_outs,
    )[:7]
    half = width // 2
    wout_value = from_blocks(sum0, width)
    key_query = from_blocks(sum1, width)
    shared = from_blocks(sum_s, 3 * hidden)
    sg, su, sd = (shared[i * hidden : (i + 1) * hidden] for i in range(3))
    return (
        output, grad_tokens, small_sums[0],
        key_query[half:], key_query[:half], wout_value[half:], wout_value[:half],
        small_sums[1], tg.T[None], tu.T[None], td[None], sg.T, su.T, sd,
        grad_logits.T, small_sums[2, :n].astype(jnp.int32),
    )


def solution(mesh):
    in_specs = (
        P(("exp", "hid"), None),
        P(),
        P("hid", None),
        P("hid", None),
        P("hid", None),
        P("hid", None),
        P(),
        P("exp", None, "hid"),
        P("exp", None, "hid"),
        P("exp", "hid", None),
        P(None, "hid"),
        P(None, "hid"),
        P("hid", None),
        P(("exp", "hid"), None),
        P(("exp", "hid"), None),
        P(("exp", "hid")),
        P(("exp", "hid"), None),
    )
    out_specs = (
        P(("exp", "hid"), None),
        P(("exp", "hid"), None),
        P(),
        P("hid", None),
        P("hid", None),
        P("hid", None),
        P("hid", None),
        P(),
        P("exp", None, "hid"),
        P("exp", None, "hid"),
        P("exp", "hid", None),
        P(None, "hid"),
        P(None, "hid"),
        P("hid", None),
        P(("exp", "hid"), None),
        P(),
    )
    return jax.shard_map(
        on_device, mesh=mesh, in_specs=in_specs, out_specs=out_specs, check_vma=False
    )
```

profile of v0, /device:TPU:0, one launch (start us, length us, event | category | flops | bytes accessed | tf_op | source)
XLA Modules:
  0.0 512.6 jit_solution(3662787475286278184)
XLA Ops:
  1.3 1.3 broadcast_in_dim.15.gain1
  2.6 1.3 broadcast_in_dim.16.gain2
  3.9 92.7 %shard_map.306 = (bf16[8,256,1280]{2,1,0:T(8,128)(2,1)}, bf16[8,256,1280]{2,1,0:T(8,128)(2,1)}, bf16[2,640,1280]{2,1,0:T(8,128)(2,1)}, bf16[2,640,1280]{2,1,0:T(...) custom-call(bf16[256,1280]{1,0:T(8,128)(2,1)} %x_ref.3, ...), custom_call_target="tpu_custom_call" | custom-call | tf_op jit(solution)/shard_map/pallas_call | solution.py:476
  96.6 213.7 %shard_map.307 = (f32[16,1,256]{2,1,0:T(1,128)}, f32[256,1280]{1,0:T(8,128)}, f32[448,1280]{1,0:T(8,128)}, f32[448,1280]{1,0:T(8,128)}, f32[448,1280]{1,0:T(8,12...) custom-call(bf16[8,256,1280]{2,1,0:T(8,128)(2,1)} %get-tuple-element, ...), custom_call_target="tpu_custom_call", output_to_operand_aliasing={{8}: (0, {})} | custom-call | tf_op jit(solution)/shard_map/pallas_call | solution.py:903
  310.3 177.9 %shard_map.308 = (bf16[256,1280]{1,0:T(8,128)(2,1)}, bf16[256,1280]{1,0:T(8,128)(2,1)}, f32[7,256]{1,0:T(8,128)}, f32[8,1280]{1,0:T(8,128)}, bf16[16,80,1280]{2,...) custom-call(bf16[256,1280]{1,0:T(8,128)(2,1)} %x_ref.3, ...), custom_call_target="tpu_custom_call" | custom-call | tf_op jit(solution)/shard_map/pallas_call | solution.py:1331
  488.2 1.2 convert_bitcast_fusion
  489.4 1.5 slice_reduce_fusion
  490.9 2.2 slice.56
  493.1 0.7 bitcast_convert_fusion
  493.8 0.0 copy-start
  493.8 0.0 copy-start.1
  493.9 3.6 fusion
  497.4 0.3 copy-done
  497.7 1.5 copy-done.1
  499.2 0.0 copy-start.6
  499.2 0.0 copy-start.5
  499.2 5.2 %fusion.1 = (f32[8,80,1280]{2,1,0:T(8,128)}, f32[8,80,1280]{2,1,0:T(8,128)}, f32[8,80,1280]{2,1,0:T(8,128)}, f32[8,80,1280]{2,1,0:T(8,128)}) fusion(bf16[16,80,1280]{2,1,0:T(8,128)(2,1)S(1)} %copy-done, bf16[16,80,1280]{2,1,0:T(8,128)(2,1)S(1)} %copy-done.1), kind=kLoop, calls=%fused_computation.7 | loop fusion | bytes 26214400 | tf_op jit(solution)/shard_map/slice | solution.py:1411
  504.4 0.0 copy-start.4
  504.4 0.0 copy-done.6
  504.4 0.8 copy.44
  505.3 0.0 copy-done.5
  505.3 0.0 copy-start.3
  505.3 0.8 copy.45
  506.1 0.4 copy-done.4
  506.5 1.4 copy.46
  507.9 0.0 copy-done.3
  507.9 0.0 copy-start.2
  507.9 1.4 copy.47
  509.3 1.1 copy-done.2
  510.3 1.4 copy.48
  511.7 0.0 copy-done.7
  511.7 0.6 copy.49
  (1 shorter events, 0.0 us)
Async XLA Ops:
  493.8 3.9 copy-start
  493.8 5.3 %copy-start.1 = (bf16[16,80,1280]{2,1,0:T(8,128)(2,1)S(1)}, bf16[16,80,1280]{2,1,0:T(8,128)(2,1)}, u32[]{:S(2)}) copy-start(bf16[16,80,1280]{2,1,0:T(8,128)(2,1)} %get-tuple-element.85) | copy-start | bytes 9830404
  499.2 5.3 %copy-start.6 = (bf16[256,1280]{1,0:T(8,128)(2,1)S(1)}, bf16[256,1280]{1,0:T(8,128)(2,1)}, u32[]{:S(2)}) copy-start(bf16[256,1280]{1,0:T(8,128)(2,1)} %get-tuple-element.119) | copy-start | bytes 1966084
  499.2 6.1 %copy-start.5 = (bf16[256,1280]{1,0:T(8,128)(2,1)S(1)}, bf16[256,1280]{1,0:T(8,128)(2,1)}, u32[]{:S(2)}) copy-start(bf16[256,1280]{1,0:T(8,128)(2,1)} %get-tuple-element.120) | copy-start | bytes 1966084
  504.4 2.0 copy-start.4
  505.3 2.6 copy-start.3
  507.9 2.5 copy-start.2
  510.3 1.4 copy-start.7
where the time goes:
time: 517 us; the launch traced here: 513 us
  Pallas kernels  484 us (94%)
  local copies, waits for them, and re-layouts  24.7 us (5%)
    pallas_call x1, Pallas kernels, experts(): pl.pallas_call(functools.partial(experts_kernel, n, slots), out_shape=(ou...  214 us
    pallas_call x1, Pallas kernels, tail(): pl.pallas_call(functools.partial(tail_kernel, n), out_shape=(out((rows, w...  178 us
    pallas_call x1, Pallas kernels, front(): pl.pallas_call(functools.partial(front_kernel, n), out_shape=(out((nz * m...  92.7 us

commit v1 on v0

--- a/solution.py
+++ b/solution.py
@@ -1206,12 +1206,16 @@
         )
         for i, stack in enumerate((stack0, stack1))
     )
-    first.start()
+    first.start_plane(0)
+    first.start_plane(1)
     shared_events[2]()
+    own_part(2, a_ref, dk_ref[...], stack1, 0)
+    for p in range(2, nz):
+        first.start_plane(p)
+    own_part(3, a_ref, dq_ref[...], stack1, 1)
+    second.start_plane(0)
+    second.start_plane(1)
     shared_events[3]()
-    own_part(2, a_ref, dk_ref[...], stack1, 0)
-    own_part(3, a_ref, dq_ref[...], stack1, 1)
-    second.start()
     fetch(wv, 1).wait()
     da = inner_cols(dv_ref[...], wbuf[1])
     fetch(wq, 1).start()
@@ -1219,6 +1223,8 @@
     da = da + inner_cols(dk_ref[...], wbuf[0])
     fetch(wq, 1).wait()
     da = da + inner_cols(dq_ref[...], wbuf[1])
+    for p in range(2, nz):
+        second.start_plane(p)
     scaled_one = da * gain1[...]
     grad_one = jnp.sum(da * n_one, axis=0, keepdims=True)
     back = r_one * (scaled_one - n_one * jnp.mean(scaled_one * n_one, axis=-1, keepdims=True))
@@ -1379,7 +1385,7 @@
     n = lax.axis_size("exp")
     hidden = s_gate.shape[1]
     cosine, sine = (jnp.asarray(table) for table in rotary_rows(rows))
-    gain1, gain2 = norm_one[None], norm_two[None]
+    gain1, gain2 = norm_one, norm_two
     logits, routes = logits.T, routes.T
     attn_w = (w_query, w_key, w_value, w_out)
     routed_w = (r_gate[0].T, r_up[0].T, r_down[0])

time: 517 us -> 515 us (level)
  no operation moved by 1% of the time
where the time goes in v1:
time: 515 us; the launch traced here: 510 us
  Pallas kernels  485 us (94%)
  local copies, waits for them, and re-layouts  22.2 us (4%)
    pallas_call x1, Pallas kernels, experts(): pl.pallas_call(functools.partial(experts_kernel, n, slots), out_shape=(ou...  214 us
    pallas_call x1, Pallas kernels, tail(): pl.pallas_call(functools.partial(tail_kernel, n), out_shape=(out((rows, w...  178 us
    pallas_call x1, Pallas kernels, front(): pl.pallas_call(functools.partial(front_kernel, n), out_shape=(out((nz * m...  92.8 us

profile of v1, /device:TPU:0, one launch (start us, length us, event | category | flops | bytes accessed | tf_op | source)
XLA Modules:
  0.0 510.2 jit_solution(9642712475750625757)
XLA Ops:
  1.3 92.8 %shard_map.306 = (bf16[8,256,1280]{2,1,0:T(8,128)(2,1)}, bf16[8,256,1280]{2,1,0:T(8,128)(2,1)}, bf16[2,640,1280]{2,1,0:T(8,128)(2,1)}, bf16[2,640,1280]{2,1,0:T(...) custom-call(bf16[256,1280]{1,0:T(8,128)(2,1)} %x_ref.3, ...), custom_call_target="tpu_custom_call" | custom-call | tf_op jit(solution)/shard_map/pallas_call | solution.py:476
  94.1 213.7 %shard_map.307 = (f32[16,1,256]{2,1,0:T(1,128)}, f32[256,1280]{1,0:T(8,128)}, f32[448,1280]{1,0:T(8,128)}, f32[448,1280]{1,0:T(8,128)}, f32[448,1280]{1,0:T(8,12...) custom-call(bf16[8,256,1280]{2,1,0:T(8,128)(2,1)} %get-tuple-element, ...), custom_call_target="tpu_custom_call", output_to_operand_aliasing={{8}: (0, {})} | custom-call | tf_op jit(solution)/shard_map/pallas_call | solution.py:903
  307.8 178.1 %shard_map.308 = (bf16[256,1280]{1,0:T(8,128)(2,1)}, bf16[256,1280]{1,0:T(8,128)(2,1)}, f32[7,256]{1,0:T(8,128)}, f32[8,1280]{1,0:T(8,128)}, bf16[16,80,1280]{2,...) custom-call(bf16[256,1280]{1,0:T(8,128)(2,1)} %x_ref.3, ...), custom_call_target="tpu_custom_call" | custom-call | tf_op jit(solution)/shard_map/pallas_call | solution.py:1337
  485.9 1.2 convert_bitcast_fusion
  487.1 1.5 slice_reduce_fusion
  488.5 2.2 slice.56
  490.7 0.7 bitcast_convert_fusion
  491.5 0.0 copy-start
  491.5 0.0 copy-start.1
  491.5 3.6 fusion
  495.1 0.3 copy-done
  495.4 1.5 copy-done.1
  496.8 0.0 copy-start.6
  496.8 0.0 copy-start.5
  496.8 5.2 %fusion.1 = (f32[8,80,1280]{2,1,0:T(8,128)}, f32[8,80,1280]{2,1,0:T(8,128)}, f32[8,80,1280]{2,1,0:T(8,128)}, f32[8,80,1280]{2,1,0:T(8,128)}) fusion(bf16[16,80,1280]{2,1,0:T(8,128)(2,1)S(1)} %copy-done, bf16[16,80,1280]{2,1,0:T(8,128)(2,1)S(1)} %copy-done.1), kind=kLoop, calls=%fused_computation.7 | loop fusion | bytes 26214400 | tf_op jit(solution)/shard_map/slice | solution.py:1417
  502.1 0.0 copy-start.4
  502.1 0.0 copy-done.6
  502.1 0.8 copy.44
  502.9 0.0 copy-done.5
  502.9 0.0 copy-start.3
  502.9 0.8 copy.45
  503.8 0.4 copy-done.4
  504.1 1.4 copy.46
  505.5 0.0 copy-done.3
  505.5 0.0 copy-start.2
  505.5 1.4 copy.47
  506.9 1.1 copy-done.2
  508.0 0.0 copy-start.7
  508.0 1.4 copy.48
  509.4 0.0 copy-done.7
  509.4 0.6 copy.49
Async XLA Ops:
  491.5 3.9 copy-start
  491.5 5.3 %copy-start.1 = (bf16[16,80,1280]{2,1,0:T(8,128)(2,1)S(1)}, bf16[16,80,1280]{2,1,0:T(8,128)(2,1)}, u32[]{:S(2)}) copy-start(bf16[16,80,1280]{2,1,0:T(8,128)(2,1)} %get-tuple-element.85) | copy-start | bytes 9830404
  496.8 5.3 %copy-start.6 = (bf16[256,1280]{1,0:T(8,128)(2,1)S(1)}, bf16[256,1280]{1,0:T(8,128)(2,1)}, u32[]{:S(2)}) copy-start(bf16[256,1280]{1,0:T(8,128)(2,1)} %get-tuple-element.119) | copy-start | bytes 1966084
  496.8 6.1 %copy-start.5 = (bf16[256,1280]{1,0:T(8,128)(2,1)S(1)}, bf16[256,1280]{1,0:T(8,128)(2,1)}, u32[]{:S(2)}) copy-start(bf16[256,1280]{1,0:T(8,128)(2,1)} %get-tuple-element.120) | copy-start | bytes 1966084
  502.1 2.0 copy-start.4
  502.9 2.6 copy-start.3
  505.5 2.5 copy-start.2
  508.0 1.4 copy-start.7

commit v2 on v1

--- a/solution.py
+++ b/solution.py
@@ -1308,7 +1308,7 @@
     loc1.start()
     get_base.wait()
     y_last()
-    run_staggered(g0.events(), g1.events(), 1)
+    run_staggered(g0.events(), g1.events(), 3)
     shared_events[-1]()
     for g in (gather_s, g0, g1):
         g.finish()

time: 515 us -> 517 us (level)
  no operation moved by 1% of the time
where the time goes in v2:
time: 517 us; the launch traced here: 513 us
  Pallas kernels  487 us (94%)
  local copies, waits for them, and re-layouts  22.2 us (4%)
    pallas_call x1, Pallas kernels, experts(): pl.pallas_call(functools.partial(experts_kernel, n, slots), out_shape=(ou...  214 us
    pallas_call x1, Pallas kernels, tail(): pl.pallas_call(functools.partial(tail_kernel, n), out_shape=(out((rows, w...  181 us
    pallas_call x1, Pallas kernels, front(): pl.pallas_call(functools.partial(front_kernel, n), out_shape=(out((nz * m...  92.8 us

profile of v2, /device:TPU:0, one launch (start us, length us, event | category | flops | bytes accessed | tf_op | source)
XLA Modules:
  0.0 512.7 jit_solution(1712206823326716607)
XLA Ops:
  1.3 92.8 %shard_map.306 = (bf16[8,256,1280]{2,1,0:T(8,128)(2,1)}, bf16[8,256,1280]{2,1,0:T(8,128)(2,1)}, bf16[2,640,1280]{2,1,0:T(8,128)(2,1)}, bf16[2,640,1280]{2,1,0:T(...) custom-call(bf16[256,1280]{1,0:T(8,128)(2,1)} %x_ref.3, ...), custom_call_target="tpu_custom_call" | custom-call | tf_op jit(solution)/shard_map/pallas_call | solution.py:476
  94.1 213.7 %shard_map.307 = (f32[16,1,256]{2,1,0:T(1,128)}, f32[256,1280]{1,0:T(8,128)}, f32[448,1280]{1,0:T(8,128)}, f32[448,1280]{1,0:T(8,128)}, f32[448,1280]{1,0:T(8,12...) custom-call(bf16[8,256,1280]{2,1,0:T(8,128)(2,1)} %get-tuple-element, ...), custom_call_target="tpu_custom_call", output_to_operand_aliasing={{8}: (0, {})} | custom-call | tf_op jit(solution)/shard_map/pallas_call | solution.py:903
  307.8 180.5 %shard_map.308 = (bf16[256,1280]{1,0:T(8,128)(2,1)}, bf16[256,1280]{1,0:T(8,128)(2,1)}, f32[7,256]{1,0:T(8,128)}, f32[8,1280]{1,0:T(8,128)}, bf16[16,80,1280]{2,...) custom-call(bf16[256,1280]{1,0:T(8,128)(2,1)} %x_ref.3, ...), custom_call_target="tpu_custom_call" | custom-call | tf_op jit(solution)/shard_map/pallas_call | solution.py:1337
  488.3 1.2 convert_bitcast_fusion
  489.5 1.5 slice_reduce_fusion
  491.0 2.2 slice.56
  493.2 0.7 bitcast_convert_fusion
  493.9 0.0 copy-start
  494.0 0.0 copy-start.1
  494.0 3.6 fusion
  497.5 0.3 copy-done
  497.8 1.5 copy-done.1
  499.3 0.0 copy-start.6
  499.3 0.0 copy-start.5
  499.3 5.2 %fusion.1 = (f32[8,80,1280]{2,1,0:T(8,128)}, f32[8,80,1280]{2,1,0:T(8,128)}, f32[8,80,1280]{2,1,0:T(8,128)}, f32[8,80,1280]{2,1,0:T(8,128)}) fusion(bf16[16,80,1280]{2,1,0:T(8,128)(2,1)S(1)} %copy-done, bf16[16,80,1280]{2,1,0:T(8,128)(2,1)S(1)} %copy-done.1), kind=kLoop, calls=%fused_computation.7 | loop fusion | bytes 26214400 | tf_op jit(solution)/shard_map/slice | solution.py:1417
  504.5 0.0 copy-start.4
  504.5 0.0 copy-done.6
  504.5 0.8 copy.44
  505.4 0.0 copy-done.5
  505.4 0.0 copy-start.3
  505.4 0.8 copy.45
  506.2 0.4 copy-done.4
  506.6 1.4 copy.46
  508.0 0.0 copy-done.3
  508.0 0.0 copy-start.2
  508.0 1.4 copy.47
  509.4 1.1 copy-done.2
  510.5 0.0 copy-start.7
  510.5 1.4 copy.48
  511.8 0.0 copy-done.7
  511.8 0.6 copy.49
Async XLA Ops:
  493.9 3.9 copy-start
  494.0 5.3 %copy-start.1 = (bf16[16,80,1280]{2,1,0:T(8,128)(2,1)S(1)}, bf16[16,80,1280]{2,1,0:T(8,128)(2,1)}, u32[]{:S(2)}) copy-start(bf16[16,80,1280]{2,1,0:T(8,128)(2,1)} %get-tuple-element.85) | copy-start | bytes 9830404
  499.3 5.3 %copy-start.6 = (bf16[256,1280]{1,0:T(8,128)(2,1)S(1)}, bf16[256,1280]{1,0:T(8,128)(2,1)}, u32[]{:S(2)}) copy-start(bf16[256,1280]{1,0:T(8,128)(2,1)} %get-tuple-element.119) | copy-start | bytes 1966084
  499.3 6.1 %copy-start.5 = (bf16[256,1280]{1,0:T(8,128)(2,1)S(1)}, bf16[256,1280]{1,0:T(8,128)(2,1)}, u32[]{:S(2)}) copy-start(bf16[256,1280]{1,0:T(8,128)(2,1)} %get-tuple-element.120) | copy-start | bytes 1966084
  504.5 2.0 copy-start.4
  505.4 2.6 copy-start.3
  508.0 2.5 copy-start.2
  510.5 1.4 copy-start.7
